TPU v7x, 32 devices: a whole 2x2x4 slice. The times are simulated.
32 devices in a mesh: query: 2 (over x), corpus: 16 (over z, y, core).
Axes of the slice: x: 2, y: 2, z: 4, core: 2. Of those that a mesh axis runs over, the one named last changes fastest.
Arguments:
- clean_feats: bfloat16 [2, 2, 512, 320], P('query', None, 'corpus'), may hold values from -6 to 6
- noise_draw: bfloat16 [2, 2, 512, 320], P('query', None, 'corpus'), may hold values from -6 to 6
- timesteps: int32 [2, 2], P('query'), may hold values from 0 to 999
- weight_in: bfloat16 [2, 320, 320], P(None, None, 'corpus'), may hold values from -0.3125 to 0.3125
- weight_ffin: bfloat16 [2, 320, 2560], P(None, None, 'corpus'), may hold values from -0.3125 to 0.3125
- weight_ffout: bfloat16 [2, 1280, 320], P(None, None, 'corpus'), may hold values from -0.15625 to 0.15625
- weight_out: bfloat16 [2, 320, 320], P(None, None, 'corpus'), may hold values from -0.3125 to 0.3125
- norm_gain: float32 [2, 320], replicated, may hold values from 0.5 to 1.5
- norm_bias: float32 [2, 320], replicated, may hold values from -3 to 3
- sketch_cin: bfloat16 [2, 3, 320, 16], replicated, may hold values from -0.3125 to 0.3125
- sketch_fin: bfloat16 [2, 1280, 16], replicated, may hold values from -0.15625 to 0.15625
- sketch_cout: bfloat16 [2, 3, 320, 16], replicated, may hold values from -0.3125 to 0.3125
- sketch_fout: bfloat16 [2, 2560, 16], replicated, may hold values from -0.125 to 0.125
- precond: float32 [8, 256, 256], P('query'), as said below
- store_grads: bfloat16 [8192, 2048], P(('query', 'corpus')), may hold values from -6 to 6
- store_scale: float32 [8192], P(('query', 'corpus')), may hold values from 0.002 to 0.03
Outputs:
- scores: float32 [2, 8192], P(None, ('query', 'corpus'))
Inputs may be any that keep to these rules, and one draw needn't show every extreme that they name: `precond`: each layer's matrix is symmetric with a diagonal between 1 and 2.
All inputs are finite; a program needn't handle non-finite values.
Results may differ from a plain program's by a relative error of at most 0.0085.
Values may be sent and summed in bfloat16 or wider, within the bound.
A program may use at most 64 MiB of HBM per device.

v0:
```python
import math
import jax
import jax.numpy as jnp
from jax import lax
from jax.sharding import PartitionSpec as P

plan_len = 1000


def noise_levels(timesteps):
    steps = jnp.arange(plan_len, dtype=jnp.float32)
    rooted = math.sqrt(0.00085) + (math.sqrt(0.012) - math.sqrt(0.00085)) * steps / (plan_len - 1)
    terms = jnp.log1p(-rooted * rooted)
    reached = jnp.arange(plan_len, dtype=jnp.int32) <= timesteps[..., None]
    picked = jnp.exp(jnp.sum(jnp.where(reached, terms, jnp.zeros_like(terms)), axis=-1))
    return (jnp.sqrt(picked), jnp.sqrt(1.0 - picked))


def gelu_parts(gate):
    cumul = 0.5 * (1.0 + jax.scipy.special.erf(gate / math.sqrt(2.0)))
    density = jnp.exp(-0.5 * gate * gate) / math.sqrt(2.0 * math.pi)
    return (gate * cumul, cumul + gate * density)


def contract_back(delta, weight):
    return lax.dot_general(
        delta, weight, (((1,), (1,)), ((), ())), preferred_element_type=jnp.float32
    )


def block_forward(residual_stream, weights, scale_gain, shift_bias):
    weight_in, weight_ffin, weight_ffout, weight_out = weights
    hidden = weight_ffout.shape[0]
    residual_reduced = residual_stream.astype(jnp.bfloat16)
    inner = jnp.dot(residual_reduced, weight_in, preferred_element_type=jnp.float32)
    centred_input = inner - jnp.mean(inner, axis=-1, keepdims=True)
    inverse_deviation = lax.rsqrt(
        jnp.mean(centred_input * centred_input, axis=-1, keepdims=True) + 1e-05
    )
    standardized_input = centred_input * inverse_deviation
    normalized_input = (standardized_input * scale_gain + shift_bias).astype(jnp.bfloat16)
    projected = jnp.dot(normalized_input, weight_ffin, preferred_element_type=jnp.float32)
    value_output = projected[:, :hidden]
    gate = projected[:, hidden:]
    gelu_result, gelu_derivative = gelu_parts(gate)
    mixed_hidden = (value_output * gelu_result).astype(jnp.bfloat16)
    inner_two = inner + jnp.dot(mixed_hidden, weight_ffout, preferred_element_type=jnp.float32)
    inner_reduced = inner_two.astype(jnp.bfloat16)
    residual_stream = residual_stream + jnp.dot(
        inner_reduced, weight_out, preferred_element_type=jnp.float32
    )
    return (
        residual_stream,
        (
            residual_reduced,
            standardized_input,
            inverse_deviation,
            normalized_input,
            value_output,
            gelu_result,
            gelu_derivative,
            mixed_hidden,
            inner_reduced,
        ),
    )


def block_backward(dstream, saved_activations, weights, scale_gain):
    weight_in, weight_ffin, weight_ffout, weight_out = weights
    (
        residual_reduced,
        standardized_input,
        inverse_deviation,
        normalized_input,
        value_output,
        gelu_result,
        gelu_derivative,
        mixed_hidden,
        inner_reduced,
    ) = saved_activations
    dout_low = dstream.astype(jnp.bfloat16)
    second_inner_gradient = contract_back(dout_low, weight_out)
    dtwo_low = second_inner_gradient.astype(jnp.bfloat16)
    dmixed = contract_back(dtwo_low, weight_ffout)
    dproj_low = jnp.concatenate(
        [dmixed * gelu_result, dmixed * value_output * gelu_derivative], axis=-1
    ).astype(jnp.bfloat16)
    dnormed = contract_back(dproj_low, weight_ffin)
    scaled_hidden = dnormed * scale_gain
    inner_gradient = second_inner_gradient + inverse_deviation * (
        scaled_hidden
        - jnp.mean(scaled_hidden, axis=-1, keepdims=True)
        - standardized_input * jnp.mean(scaled_hidden * standardized_input, axis=-1, keepdims=True)
    )
    dinner_low = inner_gradient.astype(jnp.bfloat16)
    dstream = dstream + contract_back(dinner_low, weight_in)
    records = [
        (residual_reduced, dinner_low),
        (normalized_input, dproj_low),
        (mixed_hidden, dtwo_low),
        (inner_reduced, dout_low),
    ]
    return (dstream, records)


def project_layer(inputs, deltas, sketch_in, sketch_out, samples):
    left = jnp.dot(inputs, sketch_in, preferred_element_type=jnp.float32)
    right = jnp.dot(deltas, sketch_out, preferred_element_type=jnp.float32)
    left = left.reshape(samples, -1, left.shape[-1])
    right = right.reshape(samples, -1, right.shape[-1])
    outer = jnp.einsum("srk,srj->skj", left, right, precision=lax.Precision.HIGHEST)
    return outer.reshape(samples, -1)


def sketches_of(block, sketch_cin, sketch_fin, sketch_cout, sketch_fout):
    return [
        (sketch_cin[block, 0], sketch_cout[block, 0]),
        (sketch_cin[block, 1], sketch_fout[block]),
        (sketch_fin[block], sketch_cout[block, 1]),
        (sketch_cin[block, 2], sketch_cout[block, 2]),
    ]


def on_device(
    clean_feats,
    noise_draw,
    timesteps,
    weight_in,
    weight_ffin,
    weight_ffout,
    weight_out,
    norm_gain,
    norm_bias,
    sketch_cin,
    sketch_fin,
    sketch_cout,
    sketch_fout,
    precond,
    store_grads,
    store_scale,
):
    samples = clean_feats.shape[0]
    positions = clean_feats.shape[2] * lax.axis_size("corpus")
    loss_scale = 1.0 / math.sqrt(clean_feats.shape[1] * positions)
    blocks = weight_in.shape[0]
    signal, spread = noise_levels(timesteps)
    noise_rows = noise_draw.astype(jnp.float32)
    residual_stream = (
        signal[:, :, None, None] * clean_feats.astype(jnp.float32)
        + spread[:, :, None, None] * noise_rows
    )
    residual_stream = residual_stream.reshape(-1, residual_stream.shape[-1])
    noise_rows = noise_rows.reshape(-1, noise_rows.shape[-1])
    gathered = (
        lax.all_gather(weight_in, "corpus", axis=2, tiled=True),
        lax.all_gather(weight_ffin, "corpus", axis=2, tiled=True),
        lax.all_gather(weight_ffout, "corpus", axis=2, tiled=True),
        lax.all_gather(weight_out, "corpus", axis=2, tiled=True),
    )

    def fetch_forward(block):
        return tuple((member[block] for member in gathered))

    def fetch_backward(block):
        return tuple((member[block] for member in gathered))

    saved_all = []
    for block in range(blocks):
        residual_stream, saved_activations = block_forward(
            residual_stream, fetch_forward(block), norm_gain[block], norm_bias[block]
        )
        saved_all.append(saved_activations)
    dstream = (residual_stream - noise_rows) * loss_scale
    layers = [None] * (4 * blocks)
    for block in reversed(range(blocks)):
        dstream, records = block_backward(
            dstream, saved_all[block], fetch_backward(block), norm_gain[block]
        )
        pairs = sketches_of(block, sketch_cin, sketch_fin, sketch_cout, sketch_fout)
        for index in range(4):
            layers[4 * block + index] = project_layer(
                records[index][0], records[index][1], pairs[index][0], pairs[index][1], samples
            )
    partial_grads = jnp.stack(layers, axis=1)
    totals = lax.psum(partial_grads, "corpus")
    routed = lax.all_to_all(totals, "query", split_axis=1, concat_axis=0, tiled=True)
    owned = jnp.einsum("qlk,lkj->qlj", routed, precond, precision=lax.Precision.HIGHEST).astype(
        jnp.bfloat16
    )
    preconditioned = lax.all_gather(owned, "query", axis=1, tiled=True)
    flat = preconditioned.reshape(preconditioned.shape[0], -1)
    raw = lax.dot_general(
        flat, store_grads, (((1,), (1,)), ((), ())), preferred_element_type=jnp.float32
    )
    return raw * store_scale[None, :]


def solution(mesh):
    placed = (
        P("query", None, "corpus", None),
        P("query", None, "corpus", None),
        P("query", None),
        P(None, None, "corpus"),
        P(None, None, "corpus"),
        P(None, None, "corpus"),
        P(None, None, "corpus"),
        P(),
        P(),
        P(),
        P(),
        P(),
        P(),
        P("query", None, None),
        P(("query", "corpus"), None),
        P(("query", "corpus")),
    )
    return jax.shard_map(
        on_device,
        mesh=mesh,
        in_specs=placed,
        out_specs=P(None, ("query", "corpus")),
        check_vma=False,
    )
```

profile of v0, /device:TPU:0, one launch (start us, length us, event | category | flops | bytes accessed | tf_op | source)
XLA Modules:
  0.0 167.8 jit_solution(465755251760985908)
XLA Ops:
  6.5 0.7 all-gather.5.cloned.1.call-update
  7.3 0.7 all-gather.3.cloned.1.call-update
  8.0 25.0 %all_gather.15 = bf16[2,320,320]{1,0,2:T(2,128)(2,1)S(1)} all-gather(bf16[2,320,20]{1,0,2:T(2,128)(2,1)} %param.19), channel_id=1, replica_groups=mesh['query'=2,'corpus'=16] {'corpus'}, dimensions={2}, use_global_device_ids=true | all-gather | bytes 435200 | tf_op jit(solution)/shard_map/all_gather | solution.py:155
  33.0 0.7 fusion.105
  33.7 0.9 copy.52
  34.6 19.7 %all_gather.18 = bf16[2,320,320]{1,0,2:T(2,128)(2,1)S(1)} all-gather(bf16[2,320,20]{1,0,2:T(2,128)(2,1)S(1)} %copy-done.12), channel_id=1, replica_groups=mesh['query'=2,'corpus'=16] {'corpus'}, dimensions={2}, use_global_device_ids=true | all-gather | bytes 435200 | tf_op jit(solution)/shard_map/all_gather | solution.py:158
  54.3 0.7 fusion.104
  55.0 0.9 copy.54
  55.9 0.9 copy.55
  56.8 0.9 copy.57
  57.7 0.6 slice_reduce_fusion
  58.6 0.7 fusion.102
  59.8 0.8 fusion.79
  60.7 0.6 copy-done.4
  61.3 0.8 fusion.76
  62.2 5.7 %fusion.103 = (bf16[1,1280,320]{1,0,2:T(2,128)(2,1)}, bf16[1,1280,320]{1,0,2:T(2,128)(2,1)S(1)}) fusion(bf16[2,1280,320]{1,0,2:T(2,128)(2,1)} %all-gather.5.cloned.1.call-done), kind=kLoop, calls=%fused_computation.161 | loop fusion | bytes 3276800 | tf_op jit(solution)/shard_map/slice | solution.py:162
  67.9 36.5 %all-gather.3.cloned.1.call-done = bf16[2,320,2560]{1,2,0:T(8,128)(2,1)} async-done(((bf16[2,320,160]{1,2,0:T(8,128)(2,1)}), bf16[2,320,2560]{1,2,0:T(8,128)(2,1)}) %all-gather.3.cloned.1.call-update) | async-done | bytes 3276816 | tf_op jit(solution)/shard_map/all_gather | solution.py:156
  104.3 2.5 %fusion.1 = f32[64,2560]{1,0:T(8,128)S(1)} fusion(bf16[64,320]{1,0:T(8,128)(2,1)} %copy-done.4, bf16[2,320,2560]{1,2,0:T(8,128)(2,1)} %all-gather.3.cloned.1.call-done), kind=kOutput, calls=%fused_computation.3 | convolution fusion | flops 104857600 | bytes 2670592 | tf_op jit(solution)/shard_map/dot_general | solution.py:42
  108.2 0.7 fusion.3
  116.3 32.2 %psum.7 = f32[1,8,256]{2,0,1:T(1,128)S(1)} all-reduce(f32[1,8,256]{2,0,1:T(1,128)S(1)} %constant_dynamic-update-slice_fusion), channel_id=1, replica_groups=mesh['query'=2,'corpus'=16] {'corpus'}, use_global_device_ids=true, to_apply=%region_9.10 | all-reduce | flops 2048 | bytes 16384 | tf_op jit(solution)/shard_map/psum | solution.py:185
  148.6 6.3 %all_to_all.12 = f32[1,8,256]{2,0,1:T(1,128)S(1)} all-to-all(f32[1,8,256]{2,0,1:T(1,128)S(1)} %psum.7), channel_id=1, replica_groups=mesh['query'=2,'corpus'=16] {'query'}, dimensions={1} | all-to-all | bytes 16384 | tf_op jit(solution)/shard_map/all_to_all | solution.py:186
  155.0 0.6 fusion.11
  155.6 4.3 %all_gather.19 = bf16[2,8,256]{2,0,1:T(2,128)(2,1)S(1)} all-gather(bf16[2,4,256]{2,0,1:T(2,128)(2,1)S(1)} %fusion.11), channel_id=1, replica_groups=mesh['query'=2,'corpus'=16] {'query'}, dimensions={1}, use_global_device_ids=true | all-gather | bytes 12288 | tf_op jit(solution)/shard_map/all_gather | solution.py:190
  160.0 1.0 convolution_multiply_fusion
  (119 shorter events, 9.5 us)
Async XLA Ops:
  6.5 148.5 %copy-start = (f32[4,256,256]{2,1,0:T(8,128)S(1)}, f32[4,256,256]{2,1,0:T(8,128)}, u32[]{:S(2)}) copy-start(f32[4,256,256]{2,1,0:T(8,128)} %param.29) | copy-start | bytes 3145732
  6.5 28.1 %copy-start.12 = (bf16[2,320,20]{1,0,2:T(2,128)(2,1)S(1)}, bf16[2,320,20]{1,0,2:T(2,128)(2,1)}, u32[]{:S(2)}) copy-start(bf16[2,320,20]{1,0,2:T(2,128)(2,1)} %param.22) | copy-start | bytes 76804
  6.5 55.6 %all-gather.5.cloned.1.call-start = ((), (), s32[]{:S(2)}) async-start(), calls=%async_computation.2 | async-start | bytes 1740800 | tf_op jit(solution)/shard_map/all_gather | solution.py:157
  7.3 97.1 %all-gather.3.cloned.1.call-start = ((), (), s32[]{:S(2)}) async-start(), calls=%async_computation.1 | async-start | bytes 4177920 | tf_op jit(solution)/shard_map/all_gather | solution.py:156
  54.3 3.4 %copy-start.16 = (f32[2,320]{1,0:T(2,128)S(1)}, f32[2,320]{1,0:T(2,128)}, u32[]{:S(2)}) copy-start(f32[2,320]{1,0:T(2,128)} %param.24) | copy-start | bytes 7684
  54.3 4.0 %copy-start.17 = (f32[2,320]{1,0:T(2,128)S(1)}, f32[2,320]{1,0:T(2,128)}, u32[]{:S(2)}) copy-start(f32[2,320]{1,0:T(2,128)} %param.23) | copy-start | bytes 7684
  54.3 4.0 %copy-start.21 = (s32[1,2]{1,0:T(1,128)S(1)}, s32[1,2]{1,0:T(1,128)}, u32[]{:S(2)}) copy-start(s32[1,2]{1,0:T(1,128)} %param.18) | copy-start | bytes 28
  54.3 4.3 %copy-start.6 = (bf16[1,2,32,320]{3,2,1,0:T(8,128)(2,1)S(1)}, bf16[1,2,32,320]{3,2,1,0:T(8,128)(2,1)}, u32[]{:S(2)}) copy-start(bf16[1,2,32,320]{3,2,1,0:T(8,128)(2,1)} %param.17) | copy-start | bytes 122884
  54.3 4.3 %copy-start.11 = (bf16[1,2,32,320]{3,2,1,0:T(8,128)(2,1)S(1)}, bf16[1,2,32,320]{3,2,1,0:T(8,128)(2,1)}, u32[]{:S(2)}) copy-start(bf16[1,2,32,320]{3,2,1,0:T(8,128)(2,1)} %param.16) | copy-start | bytes 122884
  59.6 8.3 %copy-start.14 = (f32[64]{0:T(128)}, f32[64]{0:T(128)S(1)}, u32[]{:S(2)}) copy-start(f32[64]{0:T(128)S(1)} %broadcast_multiply_fusion.5) | copy-start | bytes 772
  59.8 2.4 %copy-start.18 = (f32[64]{0:T(128)}, f32[64]{0:T(128)S(1)}, u32[]{:S(2)}) copy-start(f32[64]{0:T(128)S(1)} %add_rsqrt_fusion.1) | copy-start | bytes 772
  104.3 2.9 %copy-start.10 = (bf16[2,3,320,16]{2,3,1,0:T(8,128)(2,1)S(1)}, bf16[2,3,320,16]{2,3,1,0:T(8,128)(2,1)}, u32[]{:S(2)}) copy-start(bf16[2,3,320,16]{2,3,1,0:T(8,128)(2,1)} %param.25) | copy-start | bytes 184324
  104.3 3.1 %copy-start.5 = (f32[1,2,32,320]{3,2,1,0:T(8,128)S(1)}, f32[1,2,32,320]{3,2,1,0:T(8,128)}, u32[]{:S(2)}) copy-start(f32[1,2,32,320]{3,2,1,0:T(8,128)} %get-tuple-element.14) | copy-start | bytes 245764
  104.3 3.9 %copy-start.1 = (bf16[2,320,2560]{1,2,0:T(8,128)(2,1)S(1)}, bf16[2,320,2560]{1,2,0:T(8,128)(2,1)}, u32[]{:S(2)}) copy-start(bf16[2,320,2560]{1,2,0:T(8,128)(2,1)} %all-gather.3.cloned.1.call-done) | copy-start | bytes 9830404
  106.8 1.3 copy-start.13
  107.9 1.4 copy-start.2
  108.2 1.5 copy-start.7
  110.9 0.9 copy-start.9
  110.9 1.6 copy-start.8
  111.3 2.0 %copy-start.22 = (bf16[2,2560,16]{1,2,0:T(8,128)(2,1)S(1)}, bf16[2,2560,16]{1,2,0:T(8,128)(2,1)}, u32[]{:S(2)}) copy-start(bf16[2,2560,16]{1,2,0:T(8,128)(2,1)} %param.28) | copy-start | bytes 491524
  111.5 2.2 %copy-start.15 = (f32[64]{0:T(128)S(1)}, f32[64]{0:T(128)}, u32[]{:S(2)}) copy-start(f32[64]{0:T(128)} %copy-done.14) | copy-start | bytes 772
  111.5 2.2 %copy-start.19 = (f32[64]{0:T(128)S(1)}, f32[64]{0:T(128)}, u32[]{:S(2)}) copy-start(f32[64]{0:T(128)} %copy-done.18) | copy-start | bytes 772
  113.7 46.3 %copy-start.3 = (bf16[256,2048]{1,0:T(8,128)(2,1)S(1)}, bf16[256,2048]{1,0:T(8,128)(2,1)}, u32[]{:S(2)}) copy-start(bf16[256,2048]{1,0:T(8,128)(2,1)} %param.30) | copy-start | bytes 3145732
  113.7 46.3 %copy-start.20 = (f32[256]{0:T(256)S(1)}, f32[256]{0:T(256)}, u32[]{:S(2)}) copy-start(f32[256]{0:T(256)} %param.31) | copy-start | bytes 3076
  (1 other events, 0.6 us)
Sparse Core Ops, SparseCore 0:
  9.5 43.8 all-gather.4
  55.7 48.5 all-gather.2
where the time goes:
time: 168 us
  blocking collectives  87.6 us (52%)
  waiting for transfers between devices  37.9 us (23%)
  between operations  13.9 us (8%)
  matrix products  13.5 us (8%)
  local copies, waits for them, and re-layouts  13 us (8%)
  other arithmetic  1.84 us (1%)
    all_gather x1, waiting for transfers between devices, on_device(): lax.all_gather(weight_ffin, 'corpus', axis=2, tiled=True)  36.5 us
    psum x1, blocking collectives, on_device(): totals = lax.psum(partial_grads, 'corpus')  32.2 us
    all_gather x1, blocking collectives, on_device(): lax.all_gather(weight_in, 'corpus', axis=2, tiled=True)  25 us
    all_gather x1, blocking collectives, on_device(): lax.all_gather(weight_out, 'corpus', axis=2, tiled=True)  19.7 us
    slice x3, local copies, waits for them, and re-layouts, fetch_forward(): return tuple((member[block] for member in gathered))  7.04 us
    all_to_all x1, blocking collectives, on_device(): lax.all_to_all(totals, 'query', split_axis=1, concat_axis=0, tiled=True)  6.35 us
    unnamed x57, local copies, waits for them, and re-layouts  4.61 us
    all_gather x1, blocking collectives, on_device(): preconditioned = lax.all_gather(owned, 'query', axis=1, tiled=True)  4.33 us
  transfers between devices with their start and end apart: 2, of which 1 were waited for; matrix products, arithmetic and copies ran while one was open for 9% of the time, Pallas kernels for 0%

commit v1 on v0

--- a/solution.py
+++ b/solution.py
@@ -5,6 +5,27 @@
 from jax.sharding import PartitionSpec as P
 
 plan_len = 1000
+
+
+def collect(x, axis, dim):
+    size, index, extent = (lax.axis_size(axis), lax.axis_index(axis), x.shape[dim])
+    ahead = [(i, (i + 1) % size) for i in range(size)]
+    left = [(i, (i - 1) % size) for i in range(size)]
+    whole = jnp.zeros((*x.shape[:dim], size * extent, *x.shape[dim + 1 :]), x.dtype)
+    whole = lax.dynamic_update_slice_in_dim(whole, x, index * extent, axis=dim)
+    from_left = from_right = x
+    middle = size // 2
+    for step in range(1, middle + 1):
+        from_left = lax.ppermute(from_left, axis, ahead)
+        whole = lax.dynamic_update_slice_in_dim(
+            whole, from_left, (index - step) % size * extent, axis=dim
+        )
+        if step < size - middle:
+            from_right = lax.ppermute(from_right, axis, left)
+            whole = lax.dynamic_update_slice_in_dim(
+                whole, from_right, (index + step) % size * extent, axis=dim
+            )
+    return whole
 
 
 def noise_levels(timesteps):
@@ -153,7 +174,7 @@
     noise_rows = noise_rows.reshape(-1, noise_rows.shape[-1])
     gathered = (
         lax.all_gather(weight_in, "corpus", axis=2, tiled=True),
-        lax.all_gather(weight_ffin, "corpus", axis=2, tiled=True),
+        collect(weight_ffin, "corpus", 2),
         lax.all_gather(weight_ffout, "corpus", axis=2, tiled=True),
         lax.all_gather(weight_out, "corpus", axis=2, tiled=True),
     )

time: 168 us -> 186 us (1.11)
  starting transfers between devices: 0.04 us -> 32.3 us
  waiting for transfers between devices: 37.9 us -> 29.9 us
  blocking collectives: 87.6 us -> 81 us
  matrix products: 13.5 us -> 10.3 us
  local copies, waits for them, and re-layouts: 13 us -> 15.3 us
    all_gather x1 -> x0, waiting for transfers between devices: 36.5 us -> none  [on_device(): lax.all_gather(weight_ffin, 'corpus', axis=2, tiled=True)]
    ppermute x0 -> x15, starting transfers between devices: none -> 32.2 us  [the longest x7 31.4 us: collect(): from_right = lax.ppermute(from_right, axis, left)]
    ppermute x0 -> x15, waiting for transfers between devices: none -> 29.8 us  [the longest x8 29.8 us: collect(): from_left = lax.ppermute(from_left, axis, ahead)]
    all_gather x1, blocking collectives: 25 us -> 21.2 us  [on_device(): lax.all_gather(weight_in, 'corpus', axis=2, tiled=True)]
    dynamic_update_slice x0 -> x16, local copies, waits for them, and re-layouts: none -> 2.57 us  [the longest x7 1.26 us: collect(): lax.dynamic_update_slice_in_dim(whole, from_right, (index + step) % size...]
    psum x1, blocking collectives: 32.2 us -> 30 us  [on_device(): totals = lax.psum(partial_grads, 'corpus')]
    unnamed x57 -> x39, local copies, waits for them, and re-layouts: 4.61 us -> 5.54 us
  transfers between devices with their start and end apart: 2 -> 16, of which waited for: 1 -> 7; matrix products, arithmetic and copies ran while one was open for 9% -> 6% of each run, Pallas kernels for 0% -> 0%
where the time goes in v1:
time: 186 us
  blocking collectives  81 us (44%)
  starting transfers between devices  32.3 us (17%)
  waiting for transfers between devices  29.9 us (16%)
  local copies, waits for them, and re-layouts  15.3 us (8%)
  between operations  14.3 us (8%)
  matrix products  10.3 us (6%)
  other arithmetic  2.66 us (1%)
    ppermute x7, starting transfers between devices, collect(): from_right = lax.ppermute(from_right, axis, left)  31.4 us
    psum x1, blocking collectives, on_device(): totals = lax.psum(partial_grads, 'corpus')  30 us
    ppermute x8, waiting for transfers between devices, collect(): from_left = lax.ppermute(from_left, axis, ahead)  29.8 us
    all_gather x1, blocking collectives, on_device(): lax.all_gather(weight_in, 'corpus', axis=2, tiled=True)  21.2 us
    all_gather x1, blocking collectives, on_device(): lax.all_gather(weight_out, 'corpus', axis=2, tiled=True)  19.1 us
    all_to_all x1, blocking collectives, on_device(): lax.all_to_all(totals, 'query', split_axis=1, concat_axis=0, tiled=True)  6.36 us
    slice x3, local copies, waits for them, and re-layouts, fetch_forward(): return tuple((member[block] for member in gathered))  6.1 us
    unnamed x39, local copies, waits for them, and re-layouts  5.54 us
  transfers between devices with their start and end apart: 16, of which 7 were waited for; matrix products, arithmetic and copies ran while one was open for 6% of the time, Pallas kernels for 0%

profile of v1, /device:TPU:0, one launch (start us, length us, event | category | flops | bytes accessed | tf_op | source)
XLA Modules:
  0.0 185.8 jit_solution(10408542153390276865)
XLA Ops:
  7.1 5.1 %collective-permute-start.1 = (bf16[2,320,160]{1,2,0:T(8,128)(2,1)}, bf16[2,320,160]{1,2,0:T(8,128)(2,1)}, u32[]{:S(2)}, u32[]{:S(2)}) collective-permute-start(bf16[2,320,160]{1,2,0:T(8,128)(2,1)} %param.20), channel_id=1, source_target_pairs={{0,15},{1,0},{2,1},{3,2},{4,3},{5,4},{6,5},{7,6},{8,7},{9,8},{10,9... | collective-permute-start | bytes 614408 | tf_op jit(solution)/shard_map/ppermute | solution.py:24
  13.3 21.2 %all_gather.12 = bf16[2,320,320]{1,0,2:T(2,128)(2,1)S(1)} all-gather(bf16[2,320,20]{1,0,2:T(2,128)(2,1)} %param.19), channel_id=1, replica_groups=mesh['query'=2,'corpus'=16] {'corpus'}, dimensions={2}, use_global_device_ids=true | all-gather | bytes 435200 | tf_op jit(solution)/shard_map/all_gather | solution.py:176
  37.7 19.1 %all_gather.14 = bf16[2,320,320]{1,0,2:T(2,128)(2,1)S(1)} all-gather(bf16[2,320,20]{1,0,2:T(2,128)(2,1)S(1)} %copy-done.9), channel_id=1, replica_groups=mesh['query'=2,'corpus'=16] {'corpus'}, dimensions={2}, use_global_device_ids=true | all-gather | bytes 435200 | tf_op jit(solution)/shard_map/all_gather | solution.py:179
  61.3 4.1 %collective-permute-start.3 = (bf16[2,320,160]{1,2,0:T(8,128)(2,1)}, bf16[2,320,160]{1,2,0:T(8,128)(2,1)S(1)}, u32[]{:S(2)}, u32[]{:S(2)}) collective-permute-start(bf16[2,320,160]{1,2,0:T(8,128)(2,1)} %collective-permute-done.1), channel_id=1, source_target_pairs={{0,15},{1,0},{2,1},{3,2},{4,3},{5,4},{6,5},{7,6},{8,7},{9,8},{10,9... | collective-permute-start | bytes 614408 | tf_op jit(solution)/shard_map/ppermute | solution.py:24
  65.4 1.0 constant_dynamic-update-slice_fusion.22
  66.4 1.0 constant_dynamic-update-slice_fusion.21
  67.4 2.2 %collective-permute-done.2 = bf16[2,320,160]{1,2,0:T(8,128)(2,1)S(1)} collective-permute-done((bf16[2,320,160]{1,2,0:T(8,128)(2,1)}, bf16[2,320,160]{1,2,0:T(8,128)(2,1)S(1)}, u32[]{:S(2)}, u32[]{:S(2)}) %collective-permute-start.2) | collective-permute-done | bytes 204832 | tf_op jit(solution)/shard_map/ppermute | solution.py:19
  69.6 4.4 %collective-permute-start.5 = (bf16[2,320,160]{1,2,0:T(8,128)(2,1)S(1)}, bf16[2,320,160]{1,2,0:T(8,128)(2,1)S(1)}, u32[]{:S(2)}, u32[]{:S(2)}) collective-permute-start(bf16[2,320,160]{1,2,0:T(8,128)(2,1)S(1)} %collective-permute-done.3), channel_id=1, source_target_pairs={{0,15},{1,0},{2,1},{3,2},{4,3},{5,4},{6,5},{7,6},{8,7},{9,8},{10,9... | collective-permute-start | bytes 614408 | tf_op jit(solution)/shard_map/ppermute | solution.py:24
  74.1 3.9 %collective-permute-done.4 = bf16[2,320,160]{1,2,0:T(8,128)(2,1)S(1)} collective-permute-done((bf16[2,320,160]{1,2,0:T(8,128)(2,1)S(1)}, bf16[2,320,160]{1,2,0:T(8,128)(2,1)S(1)}, u32[]{:S(2)}, u32[]{:S(2)}) %collective-permute-start.4) | collective-permute-done | bytes 204832 | tf_op jit(solution)/shard_map/ppermute | solution.py:19
  78.0 4.4 %collective-permute-start.7 = (bf16[2,320,160]{1,2,0:T(8,128)(2,1)S(1)}, bf16[2,320,160]{1,2,0:T(8,128)(2,1)S(1)}, u32[]{:S(2)}, u32[]{:S(2)}) collective-permute-start(bf16[2,320,160]{1,2,0:T(8,128)(2,1)S(1)} %collective-permute-done.5), channel_id=1, source_target_pairs={{0,15},{1,0},{2,1},{3,2},{4,3},{5,4},{6,5},{7,6},{8,7},{9,8},{10,9... | collective-permute-start | bytes 614408 | tf_op jit(solution)/shard_map/ppermute | solution.py:24
  82.6 3.9 %collective-permute-done.6 = bf16[2,320,160]{1,2,0:T(8,128)(2,1)S(1)} collective-permute-done((bf16[2,320,160]{1,2,0:T(8,128)(2,1)S(1)}, bf16[2,320,160]{1,2,0:T(8,128)(2,1)S(1)}, u32[]{:S(2)}, u32[]{:S(2)}) %collective-permute-start.6) | collective-permute-done | bytes 204832 | tf_op jit(solution)/shard_map/ppermute | solution.py:19
  86.4 4.4 %collective-permute-start.9 = (bf16[2,320,160]{1,2,0:T(8,128)(2,1)S(1)}, bf16[2,320,160]{1,2,0:T(8,128)(2,1)S(1)}, u32[]{:S(2)}, u32[]{:S(2)}) collective-permute-start(bf16[2,320,160]{1,2,0:T(8,128)(2,1)S(1)} %collective-permute-done.7), channel_id=1, source_target_pairs={{0,15},{1,0},{2,1},{3,2},{4,3},{5,4},{6,5},{7,6},{8,7},{9,8},{10,9... | collective-permute-start | bytes 614408 | tf_op jit(solution)/shard_map/ppermute | solution.py:24
  91.0 3.9 %collective-permute-done.8 = bf16[2,320,160]{1,2,0:T(8,128)(2,1)S(1)} collective-permute-done((bf16[2,320,160]{1,2,0:T(8,128)(2,1)S(1)}, bf16[2,320,160]{1,2,0:T(8,128)(2,1)S(1)}, u32[]{:S(2)}, u32[]{:S(2)}) %collective-permute-start.8) | collective-permute-done | bytes 204832 | tf_op jit(solution)/shard_map/ppermute | solution.py:19
  94.9 4.4 %collective-permute-start.11 = (bf16[2,320,160]{1,2,0:T(8,128)(2,1)S(1)}, bf16[2,320,160]{1,2,0:T(8,128)(2,1)S(1)}, u32[]{:S(2)}, u32[]{:S(2)}) collective-permute-start(bf16[2,320,160]{1,2,0:T(8,128)(2,1)S(1)} %collective-permute-done.9), channel_id=1, source_target_pairs={{0,15},{1,0},{2,1},{3,2},{4,3},{5,4},{6,5},{7,6},{8,7},{9,8},{10,9... | collective-permute-start | bytes 614408 | tf_op jit(solution)/shard_map/ppermute | solution.py:24
  99.4 3.9 %collective-permute-done.10 = bf16[2,320,160]{1,2,0:T(8,128)(2,1)S(1)} collective-permute-done((bf16[2,320,160]{1,2,0:T(8,128)(2,1)S(1)}, bf16[2,320,160]{1,2,0:T(8,128)(2,1)S(1)}, u32[]{:S(2)}, u32[]{:S(2)}) %collective-permute-start.10) | collective-permute-done | bytes 204832 | tf_op jit(solution)/shard_map/ppermute | solution.py:19
  103.3 4.4 %collective-permute-start.13 = (bf16[2,320,160]{1,2,0:T(8,128)(2,1)S(1)}, bf16[2,320,160]{1,2,0:T(8,128)(2,1)S(1)}, u32[]{:S(2)}, u32[]{:S(2)}) collective-permute-start(bf16[2,320,160]{1,2,0:T(8,128)(2,1)S(1)} %collective-permute-done.11), channel_id=1, source_target_pairs={{0,15},{1,0},{2,1},{3,2},{4,3},{5,4},{6,5},{7,6},{8,7},{9,8},{10,9... | collective-permute-start | bytes 614408 | tf_op jit(solution)/shard_map/ppermute | solution.py:24
  107.8 3.9 %collective-permute-done.12 = bf16[2,320,160]{1,2,0:T(8,128)(2,1)S(1)} collective-permute-done((bf16[2,320,160]{1,2,0:T(8,128)(2,1)S(1)}, bf16[2,320,160]{1,2,0:T(8,128)(2,1)S(1)}, u32[]{:S(2)}, u32[]{:S(2)}) %collective-permute-start.12) | collective-permute-done | bytes 204832 | tf_op jit(solution)/shard_map/ppermute | solution.py:19
  111.8 8.2 %collective-permute-done.14 = bf16[2,320,160]{1,2,0:T(8,128)(2,1)S(1)} collective-permute-done((bf16[2,320,160]{1,2,0:T(8,128)(2,1)S(1)}, bf16[2,320,160]{1,2,0:T(8,128)(2,1)S(1)}, u32[]{:S(2)}, u32[]{:S(2)}) %collective-permute-start.14) | collective-permute-done | bytes 204832 | tf_op jit(solution)/shard_map/ppermute | solution.py:19
  120.1 1.9 %copy-done.1 = bf16[2,320,2560]{1,2,0:T(8,128)(2,1)} copy-done((bf16[2,320,2560]{1,2,0:T(8,128)(2,1)}, bf16[2,320,2560]{1,2,0:T(8,128)(2,1)S(1)}, u32[]{:S(2)}) %copy-start.1) | copy-done | bytes 3276824
  122.9 4.7 %fusion.103 = (bf16[1,1280,320]{1,0,2:T(2,128)(2,1)S(1)}, bf16[1,1280,320]{1,0,2:T(2,128)(2,1)S(1)}) fusion(bf16[2,1280,320]{1,0,2:T(2,128)(2,1)} %all-gather.2.cloned.1.call-done), kind=kLoop, calls=%fused_computation.177 | loop fusion | bytes 3276800 | tf_op jit(solution)/shard_map/slice | solution.py:183
  136.6 30.0 %psum.7 = f32[1,8,256]{2,0,1:T(1,128)S(1)} all-reduce(f32[1,8,256]{2,0,1:T(1,128)S(1)} %constant_dynamic-update-slice_fusion), channel_id=1, replica_groups=mesh['query'=2,'corpus'=16] {'corpus'}, use_global_device_ids=true, to_apply=%region_9.10 | all-reduce | flops 2048 | bytes 16384 | tf_op jit(solution)/shard_map/psum | solution.py:206
  166.6 6.4 %all_to_all.12 = f32[1,8,256]{2,0,1:T(1,128)S(1)} all-to-all(f32[1,8,256]{2,0,1:T(1,128)S(1)} %psum.7), channel_id=1, replica_groups=mesh['query'=2,'corpus'=16] {'query'}, dimensions={1} | all-to-all | bytes 16384 | tf_op jit(solution)/shard_map/all_to_all | solution.py:207
  173.6 4.3 %all_gather.15 = bf16[2,8,256]{2,0,1:T(2,128)(2,1)S(1)} all-gather(bf16[2,4,256]{2,0,1:T(2,128)(2,1)S(1)} %fusion.11), channel_id=1, replica_groups=mesh['query'=2,'corpus'=16] {'query'}, dimensions={1}, use_global_device_ids=true | all-gather | bytes 12288 | tf_op jit(solution)/shard_map/all_gather | solution.py:211
  178.0 1.0 convolution_multiply_fusion
  (145 shorter events, 19.8 us)
Async XLA Ops:
  6.5 166.5 %copy-start = (f32[4,256,256]{2,1,0:T(8,128)S(1)}, f32[4,256,256]{2,1,0:T(8,128)}, u32[]{:S(2)}) copy-start(f32[4,256,256]{2,1,0:T(8,128)} %param.29) | copy-start | bytes 3145732
  6.5 30.5 %copy-start.8 = (bf16[2,3,320,16]{2,3,1,0:T(8,128)(2,1)S(1)}, bf16[2,3,320,16]{2,3,1,0:T(8,128)(2,1)}, u32[]{:S(2)}) copy-start(bf16[2,3,320,16]{2,3,1,0:T(8,128)(2,1)} %param.25) | copy-start | bytes 184324
  6.5 30.9 %copy-start.10 = (f32[2,320]{1,0:T(2,128)S(1)}, f32[2,320]{1,0:T(2,128)}, u32[]{:S(2)}) copy-start(f32[2,320]{1,0:T(2,128)} %param.24) | copy-start | bytes 7684
  6.5 31.0 %copy-start.11 = (f32[2,320]{1,0:T(2,128)S(1)}, f32[2,320]{1,0:T(2,128)}, u32[]{:S(2)}) copy-start(f32[2,320]{1,0:T(2,128)} %param.23) | copy-start | bytes 7684
  6.5 31.2 %copy-start.9 = (bf16[2,320,20]{1,0,2:T(2,128)(2,1)S(1)}, bf16[2,320,20]{1,0,2:T(2,128)(2,1)}, u32[]{:S(2)}) copy-start(bf16[2,320,20]{1,0,2:T(2,128)(2,1)} %param.22) | copy-start | bytes 76804
  6.5 116.4 %all-gather.2.cloned.1.call-start = ((), (), s32[]{:S(2)}) async-start(), calls=%async_computation.1 | async-start | bytes 1740800 | tf_op jit(solution)/shard_map/all_gather | solution.py:178
  6.6 54.3 %collective-permute-start = (bf16[2,320,160]{1,2,0:T(8,128)(2,1)}, bf16[2,320,160]{1,2,0:T(8,128)(2,1)}, u32[]{:S(2)}, u32[]{:S(2)}) collective-permute-start(bf16[2,320,160]{1,2,0:T(8,128)(2,1)} %param.20), channel_id=1, source_target_pairs={{0,1},{1,2},{2,3},{3,4},{4,5},{5,6},{6,7},{7,8},{8,9},{9,10},{10,1... | collective-permute-start | bytes 614408 | tf_op jit(solution)/shard_map/ppermute | solution.py:19
  7.1 54.2 %collective-permute-start.1 = (bf16[2,320,160]{1,2,0:T(8,128)(2,1)}, bf16[2,320,160]{1,2,0:T(8,128)(2,1)}, u32[]{:S(2)}, u32[]{:S(2)}) collective-permute-start(bf16[2,320,160]{1,2,0:T(8,128)(2,1)} %param.20), channel_id=1, source_target_pairs={{0,15},{1,0},{2,1},{3,2},{4,3},{5,4},{6,5},{7,6},{8,7},{9,8},{10,9... | collective-permute-start | bytes 614408 | tf_op jit(solution)/shard_map/ppermute | solution.py:24
  60.9 8.7 %collective-permute-start.2 = (bf16[2,320,160]{1,2,0:T(8,128)(2,1)}, bf16[2,320,160]{1,2,0:T(8,128)(2,1)S(1)}, u32[]{:S(2)}, u32[]{:S(2)}) collective-permute-start(bf16[2,320,160]{1,2,0:T(8,128)(2,1)} %collective-permute-done), channel_id=1, source_target_pairs={{0,1},{1,2},{2,3},{3,4},{4,5},{5,6},{6,7},{7,8},{8,9},{9,10},{10,1... | collective-permute-start | bytes 614408 | tf_op jit(solution)/shard_map/ppermute | solution.py:19
  61.3 8.3 %collective-permute-start.3 = (bf16[2,320,160]{1,2,0:T(8,128)(2,1)}, bf16[2,320,160]{1,2,0:T(8,128)(2,1)S(1)}, u32[]{:S(2)}, u32[]{:S(2)}) collective-permute-start(bf16[2,320,160]{1,2,0:T(8,128)(2,1)} %collective-permute-done.1), channel_id=1, source_target_pairs={{0,15},{1,0},{2,1},{3,2},{4,3},{5,4},{6,5},{7,6},{8,7},{9,8},{10,9... | collective-permute-start | bytes 614408 | tf_op jit(solution)/shard_map/ppermute | solution.py:24
  69.6 8.4 %collective-permute-start.4 = (bf16[2,320,160]{1,2,0:T(8,128)(2,1)S(1)}, bf16[2,320,160]{1,2,0:T(8,128)(2,1)S(1)}, u32[]{:S(2)}, u32[]{:S(2)}) collective-permute-start(bf16[2,320,160]{1,2,0:T(8,128)(2,1)S(1)} %collective-permute-done.2), channel_id=1, source_target_pairs={{0,1},{1,2},{2,3},{3,4},{4,5},{5,6},{6,7},{7,8},{8,9},{9,10},{10,1... | collective-permute-start | bytes 614408 | tf_op jit(solution)/shard_map/ppermute | solution.py:19
  69.6 8.4 %collective-permute-start.5 = (bf16[2,320,160]{1,2,0:T(8,128)(2,1)S(1)}, bf16[2,320,160]{1,2,0:T(8,128)(2,1)S(1)}, u32[]{:S(2)}, u32[]{:S(2)}) collective-permute-start(bf16[2,320,160]{1,2,0:T(8,128)(2,1)S(1)} %collective-permute-done.3), channel_id=1, source_target_pairs={{0,15},{1,0},{2,1},{3,2},{4,3},{5,4},{6,5},{7,6},{8,7},{9,8},{10,9... | collective-permute-start | bytes 614408 | tf_op jit(solution)/shard_map/ppermute | solution.py:24
  78.0 8.4 %collective-permute-start.6 = (bf16[2,320,160]{1,2,0:T(8,128)(2,1)S(1)}, bf16[2,320,160]{1,2,0:T(8,128)(2,1)S(1)}, u32[]{:S(2)}, u32[]{:S(2)}) collective-permute-start(bf16[2,320,160]{1,2,0:T(8,128)(2,1)S(1)} %collective-permute-done.4), channel_id=1, source_target_pairs={{0,1},{1,2},{2,3},{3,4},{4,5},{5,6},{6,7},{7,8},{8,9},{9,10},{10,1... | collective-permute-start | bytes 614408 | tf_op jit(solution)/shard_map/ppermute | solution.py:19
  78.0 8.4 %collective-permute-start.7 = (bf16[2,320,160]{1,2,0:T(8,128)(2,1)S(1)}, bf16[2,320,160]{1,2,0:T(8,128)(2,1)S(1)}, u32[]{:S(2)}, u32[]{:S(2)}) collective-permute-start(bf16[2,320,160]{1,2,0:T(8,128)(2,1)S(1)} %collective-permute-done.5), channel_id=1, source_target_pairs={{0,15},{1,0},{2,1},{3,2},{4,3},{5,4},{6,5},{7,6},{8,7},{9,8},{10,9... | collective-permute-start | bytes 614408 | tf_op jit(solution)/shard_map/ppermute | solution.py:24
  82.6 40.2 %copy-start.6 = (bf16[2,1280,16]{1,2,0:T(8,128)(2,1)S(1)}, bf16[2,1280,16]{1,2,0:T(8,128)(2,1)}, u32[]{:S(2)}) copy-start(bf16[2,1280,16]{1,2,0:T(8,128)(2,1)} %param.26) | copy-start | bytes 245764
  86.4 8.4 %collective-permute-start.8 = (bf16[2,320,160]{1,2,0:T(8,128)(2,1)S(1)}, bf16[2,320,160]{1,2,0:T(8,128)(2,1)S(1)}, u32[]{:S(2)}, u32[]{:S(2)}) collective-permute-start(bf16[2,320,160]{1,2,0:T(8,128)(2,1)S(1)} %collective-permute-done.6), channel_id=1, source_target_pairs={{0,1},{1,2},{2,3},{3,4},{4,5},{5,6},{6,7},{7,8},{8,9},{9,10},{10,1... | collective-permute-start | bytes 614408 | tf_op jit(solution)/shard_map/ppermute | solution.py:19
  86.4 8.4 %collective-permute-start.9 = (bf16[2,320,160]{1,2,0:T(8,128)(2,1)S(1)}, bf16[2,320,160]{1,2,0:T(8,128)(2,1)S(1)}, u32[]{:S(2)}, u32[]{:S(2)}) collective-permute-start(bf16[2,320,160]{1,2,0:T(8,128)(2,1)S(1)} %collective-permute-done.7), channel_id=1, source_target_pairs={{0,15},{1,0},{2,1},{3,2},{4,3},{5,4},{6,5},{7,6},{8,7},{9,8},{10,9... | collective-permute-start | bytes 614408 | tf_op jit(solution)/shard_map/ppermute | solution.py:24
  94.9 8.4 %collective-permute-start.10 = (bf16[2,320,160]{1,2,0:T(8,128)(2,1)S(1)}, bf16[2,320,160]{1,2,0:T(8,128)(2,1)S(1)}, u32[]{:S(2)}, u32[]{:S(2)}) collective-permute-start(bf16[2,320,160]{1,2,0:T(8,128)(2,1)S(1)} %collective-permute-done.8), channel_id=1, source_target_pairs={{0,1},{1,2},{2,3},{3,4},{4,5},{5,6},{6,7},{7,8},{8,9},{9,10},{10,1... | collective-permute-start | bytes 614408 | tf_op jit(solution)/shard_map/ppermute | solution.py:19
  94.9 8.4 %collective-permute-start.11 = (bf16[2,320,160]{1,2,0:T(8,128)(2,1)S(1)}, bf16[2,320,160]{1,2,0:T(8,128)(2,1)S(1)}, u32[]{:S(2)}, u32[]{:S(2)}) collective-permute-start(bf16[2,320,160]{1,2,0:T(8,128)(2,1)S(1)} %collective-permute-done.9), channel_id=1, source_target_pairs={{0,15},{1,0},{2,1},{3,2},{4,3},{5,4},{6,5},{7,6},{8,7},{9,8},{10,9... | collective-permute-start | bytes 614408 | tf_op jit(solution)/shard_map/ppermute | solution.py:24
  103.3 8.4 %collective-permute-start.12 = (bf16[2,320,160]{1,2,0:T(8,128)(2,1)S(1)}, bf16[2,320,160]{1,2,0:T(8,128)(2,1)S(1)}, u32[]{:S(2)}, u32[]{:S(2)}) collective-permute-start(bf16[2,320,160]{1,2,0:T(8,128)(2,1)S(1)} %collective-permute-done.10), channel_id=1, source_target_pairs={{0,1},{1,2},{2,3},{3,4},{4,5},{5,6},{6,7},{7,8},{8,9},{9,10},{10,1... | collective-permute-start | bytes 614408 | tf_op jit(solution)/shard_map/ppermute | solution.py:19
  103.3 8.5 %collective-permute-start.13 = (bf16[2,320,160]{1,2,0:T(8,128)(2,1)S(1)}, bf16[2,320,160]{1,2,0:T(8,128)(2,1)S(1)}, u32[]{:S(2)}, u32[]{:S(2)}) collective-permute-start(bf16[2,320,160]{1,2,0:T(8,128)(2,1)S(1)} %collective-permute-done.11), channel_id=1, source_target_pairs={{0,15},{1,0},{2,1},{3,2},{4,3},{5,4},{6,5},{7,6},{8,7},{9,8},{10,9... | collective-permute-start | bytes 614408 | tf_op jit(solution)/shard_map/ppermute | solution.py:24
  111.7 8.3 %collective-permute-start.14 = (bf16[2,320,160]{1,2,0:T(8,128)(2,1)S(1)}, bf16[2,320,160]{1,2,0:T(8,128)(2,1)S(1)}, u32[]{:S(2)}, u32[]{:S(2)}) collective-permute-start(bf16[2,320,160]{1,2,0:T(8,128)(2,1)S(1)} %collective-permute-done.12), channel_id=1, source_target_pairs={{0,1},{1,2},{2,3},{3,4},{4,5},{5,6},{6,7},{7,8},{8,9},{9,10},{10,1... | collective-permute-start | bytes 614408 | tf_op jit(solution)/shard_map/ppermute | solution.py:19
  132.3 45.7 %copy-start.3 = (bf16[256,2048]{1,0:T(8,128)(2,1)S(1)}, bf16[256,2048]{1,0:T(8,128)(2,1)}, u32[]{:S(2)}) copy-start(bf16[256,2048]{1,0:T(8,128)(2,1)} %param.30) | copy-start | bytes 3145732
  132.3 45.7 %copy-start.12 = (f32[256]{0:T(256)S(1)}, f32[256]{0:T(256)}, u32[]{:S(2)}) copy-start(f32[256]{0:T(256)} %param.31) | copy-start | bytes 3076
  (6 other events, 18.1 us)
Sparse Core Ops, SparseCore 0:
  12.3 41.8 all-gather.1
